TPU v7x, 32 devices: a whole 2x2x4 slice. The times are simulated.
32 devices in a mesh: xy: 8 (over y, x, core), gz: 4 (over z).
Axes of the slice: x: 2, y: 2, z: 4, core: 2. Of those that a mesh axis runs over, the one named last changes fastest.
Arguments:
- volume: float32 [384, 8192], P('gz', 'xy'), may hold values from 0 to 1
- sinogram: float32 [384, 2048], P('gz', 'xy'), may hold values from 100 to 2000
- ray_mats: bfloat16 [8, 4, 256, 256], P('xy'), may hold values from 0.049804688 to 1
- offsets: int32 [8, 4], P('xy'), may hold values from 0 to 768
- ray_lists: int32 [8, 4], replicated, may hold values from 0 to 7, all different within a row
- owner_map: int32 [8], replicated, may hold values from 0 to 7, each once
Outputs:
- new_volume: float32 [384, 8192], P('gz', 'xy')
- weighted: float32 [384, 2048], P('gz', 'xy')
Inputs may be any that keep to these rules, and one draw needn't show every extreme that they name: `ray_lists`: the 4 entries of a row are distinct, and every ray block is named by some row. `owner_map`: each owner appears once.
All inputs are finite; a program needn't handle non-finite values.
Results may differ from a plain program's by a relative error of at most 0.0003.
Values sent between devices are 32-bit elements; how exact they have to be, the bound alone decides.
A program may use at most 64 MiB of HBM per device.

v0:
```python
import jax
import jax.numpy as jnp
from jax import lax
from jax.sharding import PartitionSpec as P

relax = 1.0
tv_weight = 0.2
smooth_sq = 0.01


def padded_2(cells, sides, width):
    for axis, dim in sides:
        count = lax.axis_size(axis)
        ends = count - 1
        head = lax.slice_in_dim(cells, 0, width, axis=dim)
        tail = lax.slice_in_dim(cells, cells.shape[dim] - width, cells.shape[dim], axis=dim)
        cells = jnp.concatenate(
            [
                lax.ppermute(tail, axis, [(i, (i + 1) % count) for i in range(ends)]),
                cells,
                lax.ppermute(head, axis, [((i + 1) % count, i) for i in range(ends)]),
            ],
            axis=dim,
        )
    return cells


def cut_windows(field, starts, width):
    return jax.vmap(lambda start: lax.dynamic_slice_in_dim(field, start, width, 1))(starts)


def spread_back(smeared, column_terms, starts, vxy):
    depth = smeared.shape[1]
    width = smeared.shape[2]

    def add_one(index, carry):
        update, column = carry
        start = starts[index]
        piece = lax.dynamic_slice_in_dim(update, start, width, 1) + smeared[index]
        update = lax.dynamic_update_slice_in_dim(update, piece, start, 1)
        col_piece = lax.dynamic_slice_in_dim(column, start, width, 0) + column_terms[index]
        column = lax.dynamic_update_slice_in_dim(column, col_piece, start, 0)
        return (update, column)

    init = (jnp.zeros((depth, vxy), jnp.float32), jnp.zeros((vxy,), jnp.float32))
    return lax.fori_loop(0, smeared.shape[0], add_one, init)


def total_variation(padded):
    diffs = padded[1:] - padded[:-1]
    slopes = diffs / jnp.sqrt(diffs * diffs + smooth_sq)
    return slopes[:-1] - slopes[1:]


def per_device(volume, sinogram, ray_mats, offsets, ray_lists, owner_map):
    faces = padded_2(volume, (("gz", 0),), 1)
    count = lax.axis_size("xy")
    myself = lax.axis_index("xy")
    labels = jnp.arange(count, dtype=jnp.int32)
    mine = lax.dynamic_index_in_dim(ray_lists, myself, 0, keepdims=False)
    owners = jnp.sum(jnp.where(mine[:, None] == labels[None, :], owner_map[None, :], 0), axis=1)
    matrix = ray_mats[0].astype(jnp.float32)
    starts = offsets[0]
    windows = cut_windows(volume, starts, matrix.shape[1])
    partial_value = jnp.einsum("kzw,kwr->kzr", windows, matrix, precision=lax.Precision.HIGHEST)
    row_terms = jnp.sum(matrix, axis=1)
    outgoing = (
        jnp.zeros((count,) + partial_value.shape[1:], jnp.float32).at[owners].set(partial_value)
    )
    out_rows = jnp.zeros((count, 1, row_terms.shape[1]), jnp.float32).at[owners, 0].set(row_terms)
    arrived, arrived_rows = (
        lax.all_to_all(outgoing, "xy", split_axis=0, concat_axis=0, tiled=True),
        lax.all_to_all(out_rows, "xy", split_axis=0, concat_axis=0, tiled=True),
    )
    projection = jnp.sum(arrived, axis=0)
    rowsum = jnp.sum(arrived_rows, axis=0)[0]
    weighted = (sinogram - projection) / rowsum[None, :]
    all_owners = jnp.sum(
        jnp.where(ray_lists[:, :, None] == labels[None, None, :], owner_map[None, None, :], 0),
        axis=2,
    )
    helpers = jnp.any(all_owners == myself, axis=1)
    returning = jnp.where(helpers[:, None, None], weighted[None], 0.0)
    returned = lax.all_to_all(returning, "xy", split_axis=0, concat_axis=0, tiled=True)
    needed = returned[owners]
    smeared = jnp.einsum("kzr,kwr->kzw", needed, matrix, precision=lax.Precision.HIGHEST)
    update, column = spread_back(smeared, jnp.sum(matrix, axis=2), starts, volume.shape[1])
    update = update / jnp.maximum(column, 1.0)[None, :]
    new_volume = volume + relax * update - tv_weight * total_variation(faces)
    return (new_volume, weighted)


def solution(mesh):
    in_specs = (P("gz", "xy"), P("gz", "xy"), P("xy", None, None, None), P("xy", None), P(), P())
    out_specs = (P("gz", "xy"), P("gz", "xy"))
    return jax.shard_map(
        per_device, mesh=mesh, in_specs=in_specs, out_specs=out_specs, check_vma=False
    )
```

profile of v0, /device:TPU:0, one launch (start us, length us, event | category | flops | bytes accessed | tf_op | source)
XLA Modules:
  0.0 76.1 jit_solution(17232710828339170209)
XLA Ops:
  0.6 0.7 copy-done.4
  2.2 1.3 %convert_reduce_fusion = (f32[4,256]{1,0:T(4,128)S(1)}, f32[4,256]{1,0:T(4,128)S(1)}) fusion(bf16[1,4,256,256]{3,2,1,0:T(8,128)(2,1)} %param.10), kind=kLoop, calls=%fused_computation.8 | loop fusion | flops 784384 | bytes 532480 | tf_op jit(solution)/shard_map/reduce_sum | solution.py:87
  3.5 0.6 scatter_custom_fusion.1
  4.1 0.6 reshape.91
  4.7 5.2 %all-to-all-start.1 = ((f32[8,1,256]{2,1,0:T(1,128)}), f32[8,1,256]{2,1,0:T(1,128)S(1)}, u32[]{:S(2)}, u32[]{:S(2)}) async-start(f32[8,1,256]{2,1,0:T(1,128)} %reshape.91), calls=%async_computation.1 | async-start | bytes 16384 | tf_op jit(solution)/shard_map/all_to_all | solution.py:73
  9.9 0.6 copy-done.6
  10.6 9.5 %while.17 = (s32[]{:T(128)}, f32[96,1024]{1,0:T(8,128)}, s32[4,2]{0,1:T(2,128)S(1)}, f32[4,96,256]{2,1,0:T(8,128)S(1)}, s32[]{:T(128)}) while((s32[]{:T(128)}, f32[96,1024]{1,0:T(8,128)}, s32[4,2]{0,1:T(2,128)S(1)}, f32[4,96,256]{2,1,0:T(8,128)S(1)}, s32[]{:T(128)}) %tuple.45), condition=%wide.while_cond, body=%wide.while_body.sunk | while | flops 2 | bytes 196705 | solution.py:29
  10.6 0.6 slice.46
  11.2 1.7 %bitcast_dynamic-update-slice_fusion.2 = f32[4,96,256]{2,1,0:T(8,128)S(1)} fusion(f32[4,96,256]{2,1,0:T(8,128)S(1)} %get-tuple-element.216, s32[]{:T(128)} %get-tuple-element.213, f32[96,1024]{1,0:T(8,128)} %get-tuple-element.219, s32[]{:T(128)} %bitcast.32), kind=kLoop, calls=%fused_computation.6.clone.1 | loop fusion | bytes 196616 | tf_op jit(solution)/shard_map/vmap()/gather
  13.6 1.7 %bitcast_dynamic-update-slice_fusion.2 = f32[4,96,256]{2,1,0:T(8,128)S(1)} fusion(f32[4,96,256]{2,1,0:T(8,128)S(1)} %get-tuple-element.216, s32[]{:T(128)} %get-tuple-element.213, f32[96,1024]{1,0:T(8,128)} %get-tuple-element.219, s32[]{:T(128)} %bitcast.32), kind=kLoop, calls=%fused_computation.6.clone.1 | loop fusion | bytes 196616 | tf_op jit(solution)/shard_map/vmap()/gather
  16.0 1.7 %bitcast_dynamic-update-slice_fusion.2 = f32[4,96,256]{2,1,0:T(8,128)S(1)} fusion(f32[4,96,256]{2,1,0:T(8,128)S(1)} %get-tuple-element.216, s32[]{:T(128)} %get-tuple-element.213, f32[96,1024]{1,0:T(8,128)} %get-tuple-element.219, s32[]{:T(128)} %bitcast.32), kind=kLoop, calls=%fused_computation.6.clone.1 | loop fusion | bytes 196616 | tf_op jit(solution)/shard_map/vmap()/gather
  18.4 1.7 %bitcast_dynamic-update-slice_fusion.2 = f32[4,96,256]{2,1,0:T(8,128)S(1)} fusion(f32[4,96,256]{2,1,0:T(8,128)S(1)} %get-tuple-element.216, s32[]{:T(128)} %get-tuple-element.213, f32[96,1024]{1,0:T(8,128)} %get-tuple-element.219, s32[]{:T(128)} %bitcast.32), kind=kLoop, calls=%fused_computation.6.clone.1 | loop fusion | bytes 196616 | tf_op jit(solution)/shard_map/vmap()/gather
  20.5 0.9 %broadcast_in_dim.72 = f32[8,96,256]{2,1,0:T(8,128)} broadcast(f32[]{:T(128)} %constant.51.clone.1), dimensions={} | broadcast | bytes 786436 | tf_op jit(solution)/shard_map/broadcast_in_dim | solution.py:68
  21.4 2.3 %scatter_fusion = f32[8,96,256]{2,1,0:T(8,128)} fusion(f32[8,96,256]{2,1,0:T(8,128)} %broadcast_in_dim.72, s32[4]{0:T(128)S(1)} %fusion.8, f32[4,96,256]{2,1,0:T(8,128)S(1)} %fusion.2), kind=kCustom, calls=%fused_computation.1 | custom fusion | bytes 1179664 | tf_op jit(solution)/shard_map/scatter | solution.py:68
  23.8 4.2 %all-to-all-start = ((f32[8,96,256]{2,1,0:T(8,128)}), f32[8,96,256]{2,1,0:T(8,128)S(1)}, u32[]{:S(2)}, u32[]{:S(2)}) async-start(f32[8,96,256]{2,1,0:T(8,128)} %scatter_fusion), calls=%async_computation | async-start | bytes 1572864 | tf_op jit(solution)/shard_map/all_to_all | solution.py:72
  28.3 12.3 %all-to-all-done = f32[8,96,256]{2,1,0:T(8,128)S(1)} async-done(((f32[8,96,256]{2,1,0:T(8,128)}), f32[8,96,256]{2,1,0:T(8,128)S(1)}, u32[]{:S(2)}, u32[]{:S(2)}) %all-to-all-start) | async-done | bytes 786464 | tf_op jit(solution)/shard_map/all_to_all | solution.py:72
  40.7 1.0 %broadcast_select_fusion = f32[8,96,256]{2,1,0:T(8,128)} fusion(f32[96,256]{1,0:T(8,128)S(1)} %subtract_divide_fusion, pred[8]{0:T(512)(128)(4,1)S(1)} %compare_reduce_fusion), kind=kLoop, calls=%fused_computation.19 | loop fusion | flops 196608 | bytes 884744 | tf_op jit(solution)/shard_map/jit(_where)/select_n | solution.py:83
  41.7 3.7 %all-to-all-start.2 = ((f32[8,96,256]{2,1,0:T(8,128)}), f32[8,96,256]{2,1,0:T(8,128)S(1)}, u32[]{:S(2)}, u32[]{:S(2)}) async-start(f32[8,96,256]{2,1,0:T(8,128)} %broadcast_select_fusion), calls=%async_computation.2 | async-start | bytes 1572864 | tf_op jit(solution)/shard_map/all_to_all | solution.py:84
  45.4 1.3 %collective-permute-start = (f32[1,1024]{1,0:T(1,128)S(1)}, f32[1,1024]{1,0:T(1,128)S(1)}, u32[]{:S(2)}, u32[]{:S(2)}) collective-permute-start(f32[1,1024]{1,0:T(1,128)S(1)} %get-tuple-element.144), channel_id=1, source_target_pairs={{1,0},{2,1},{3,2},{5,4},{6,5},{7,6},{9,8},{10,9},{11,10},{13,12},{... | collective-permute-start | bytes 12296 | tf_op jit(solution)/shard_map/ppermute | solution.py:21
  46.7 4.6 %collective-permute-start.1 = (f32[1,1024]{1,0:T(1,128)S(1)}, f32[1,1024]{1,0:T(1,128)S(1)}, u32[]{:S(2)}, u32[]{:S(2)}) collective-permute-start(f32[1,1024]{1,0:T(1,128)S(1)} %get-tuple-element.145), channel_id=1, source_target_pairs={{0,1},{1,2},{2,3},{4,5},{5,6},{6,7},{8,9},{9,10},{10,11},{12,13},{... | collective-permute-start | bytes 12296 | tf_op jit(solution)/shard_map/ppermute | solution.py:19
  51.3 1.3 %collective-permute-done.1 = f32[1,1024]{1,0:T(1,128)S(1)} collective-permute-done((f32[1,1024]{1,0:T(1,128)S(1)}, f32[1,1024]{1,0:T(1,128)S(1)}, u32[]{:S(2)}, u32[]{:S(2)}) %collective-permute-start.1) | collective-permute-done | bytes 4128 | tf_op jit(solution)/shard_map/ppermute | solution.py:19
  52.7 5.2 %all-to-all-done.2 = f32[8,96,256]{2,1,0:T(8,128)S(1)} async-done(((f32[8,96,256]{2,1,0:T(8,128)}), f32[8,96,256]{2,1,0:T(8,128)S(1)}, u32[]{:S(2)}, u32[]{:S(2)}) %all-to-all-start.2) | async-done | bytes 786464 | tf_op jit(solution)/shard_map/all_to_all | solution.py:84
  58.5 0.6 fusion
  59.2 16.0 %while.16 = (s32[]{:T(128)}, f32[96,1024]{1,0:T(8,128)S(1)}, f32[1024]{0:T(1024)S(1)}, s32[4]{0:T(128)S(1)}, f32[4,96,256]{2,1,0:T(8,128)S(1)}, /*index=5*/f32[4,256]{1,0:T(4,128)S(1)}, s32[]{:T(128)}, s32[]{:T(128)}, s32[]{:T(128)}) while((s32[]{:T(128)}, f32[96,1024]{1,0:T(8,128)S(1)}, f32[1024]{0:T(1024)S(1)}, s32[4]{0:T(128)S(1)}, ...), condition=%wide.region_10.11_spmd, body=%wide.region_9.10_spmd.sunk | while | flops 24837 | bytes 496799 | solution.py:46
  59.2 0.7 dynamic_slice.54
  62.1 1.1 %dynamic_update_slice.18 = f32[96,1024]{1,0:T(8,128)S(1)} dynamic-update-slice(f32[96,1024]{1,0:T(8,128)S(1)} %get-tuple-element.233, f32[96,256]{1,0:T(8,128)S(1)} %bitcast_add_fusion.2, s32[]{:T(128)} %constant.50.clone.1..sunk, s32[]{:T(128)S(6)} %select_n.66) | dynamic-update-slice | bytes 196612 | tf_op jit(solution)/shard_map/while/body/eval_jaxpr/dynamic_update_slice | solution.py:40
  63.3 0.7 dynamic_slice.54
  66.2 1.1 %dynamic_update_slice.18 = f32[96,1024]{1,0:T(8,128)S(1)} dynamic-update-slice(f32[96,1024]{1,0:T(8,128)S(1)} %get-tuple-element.233, f32[96,256]{1,0:T(8,128)S(1)} %bitcast_add_fusion.2, s32[]{:T(128)} %constant.50.clone.1..sunk, s32[]{:T(128)S(6)} %select_n.66) | dynamic-update-slice | bytes 196612 | tf_op jit(solution)/shard_map/while/body/eval_jaxpr/dynamic_update_slice | solution.py:40
  67.5 0.7 dynamic_slice.54
  70.3 1.1 %dynamic_update_slice.18 = f32[96,1024]{1,0:T(8,128)S(1)} dynamic-update-slice(f32[96,1024]{1,0:T(8,128)S(1)} %get-tuple-element.233, f32[96,256]{1,0:T(8,128)S(1)} %bitcast_add_fusion.2, s32[]{:T(128)} %constant.50.clone.1..sunk, s32[]{:T(128)S(6)} %select_n.66) | dynamic-update-slice | bytes 196612 | tf_op jit(solution)/shard_map/while/body/eval_jaxpr/dynamic_update_slice | solution.py:40
  71.6 0.7 dynamic_slice.54
  75.2 0.9 %fusion.5 = f32[96,1024]{1,0:T(8,128)} fusion(f32[97,1024]{1,0:T(8,128)S(1)} %rsqrt_multiply_fusion, f32[96,1024]{1,0:T(8,128)S(1)} %copy-done.1, f32[96,1024]{1,0:T(8,128)S(1)} %get-tuple-element.112, f32[1024]{0:T(1024)S(1)} %broadcast_maximum_fusion), kind=kLoop, calls=%fused_computation.18 | loop fusion | flops 491520 | bytes 1970176 | tf_op jit(solution)/shard_map/sub | solution.py:89
  (53 shorter events, 6.1 us)
Async XLA Ops:
  0.6 0.7 copy-start.4
  1.3 0.7 copy-start.5
  2.2 17.9 %copy-start = (bf16[1,4,256,256]{3,2,1,0:T(8,128)(2,1)S(1)}, bf16[1,4,256,256]{3,2,1,0:T(8,128)(2,1)}, u32[]{:S(2)}) copy-start(bf16[1,4,256,256]{3,2,1,0:T(8,128)(2,1)} %param.10) | copy-start | bytes 1572868
  4.7 19.0 %all-to-all-start.1 = ((f32[8,1,256]{2,1,0:T(1,128)}), f32[8,1,256]{2,1,0:T(1,128)S(1)}, u32[]{:S(2)}, u32[]{:S(2)}) async-start(f32[8,1,256]{2,1,0:T(1,128)} %reshape.91), calls=%async_computation.1 | async-start | bytes 16384 | tf_op jit(solution)/shard_map/all_to_all | solution.py:73
  9.9 0.7 copy-start.6
  23.8 16.8 %all-to-all-start = ((f32[8,96,256]{2,1,0:T(8,128)}), f32[8,96,256]{2,1,0:T(8,128)S(1)}, u32[]{:S(2)}, u32[]{:S(2)}) async-start(f32[8,96,256]{2,1,0:T(8,128)} %scatter_fusion), calls=%async_computation | async-start | bytes 1572864 | tf_op jit(solution)/shard_map/all_to_all | solution.py:72
  28.3 12.4 %copy-start.3 = (f32[96,256]{1,0:T(8,128)S(1)}, f32[96,256]{1,0:T(8,128)}, u32[]{:S(2)}) copy-start(f32[96,256]{1,0:T(8,128)} %param.9) | copy-start | bytes 294916
  40.7 1.0 %copy-start.2 = (f32[96,256]{1,0:T(8,128)}, f32[96,256]{1,0:T(8,128)S(1)}, u32[]{:S(2)}) copy-start(f32[96,256]{1,0:T(8,128)S(1)} %subtract_divide_fusion) | copy-start | bytes 294916
  41.7 3.7 %copy-start.1 = (f32[96,1024]{1,0:T(8,128)S(1)}, f32[96,1024]{1,0:T(8,128)}, u32[]{:S(2)}) copy-start(f32[96,1024]{1,0:T(8,128)} %get-tuple-element.250) | copy-start | bytes 1179652
  41.7 16.2 %all-to-all-start.2 = ((f32[8,96,256]{2,1,0:T(8,128)}), f32[8,96,256]{2,1,0:T(8,128)S(1)}, u32[]{:S(2)}, u32[]{:S(2)}) async-start(f32[8,96,256]{2,1,0:T(8,128)} %broadcast_select_fusion), calls=%async_computation.2 | async-start | bytes 1572864 | tf_op jit(solution)/shard_map/all_to_all | solution.py:84
  45.4 5.9 %collective-permute-start = (f32[1,1024]{1,0:T(1,128)S(1)}, f32[1,1024]{1,0:T(1,128)S(1)}, u32[]{:S(2)}, u32[]{:S(2)}) collective-permute-start(f32[1,1024]{1,0:T(1,128)S(1)} %get-tuple-element.144), channel_id=1, source_target_pairs={{1,0},{2,1},{3,2},{5,4},{6,5},{7,6},{9,8},{10,9},{11,10},{13,12},{... | collective-permute-start | bytes 12296 | tf_op jit(solution)/shard_map/ppermute | solution.py:21
  46.7 5.9 %collective-permute-start.1 = (f32[1,1024]{1,0:T(1,128)S(1)}, f32[1,1024]{1,0:T(1,128)S(1)}, u32[]{:S(2)}, u32[]{:S(2)}) collective-permute-start(f32[1,1024]{1,0:T(1,128)S(1)} %get-tuple-element.145), channel_id=1, source_target_pairs={{0,1},{1,2},{2,3},{4,5},{5,6},{6,7},{8,9},{9,10},{10,11},{12,13},{... | collective-permute-start | bytes 12296 | tf_op jit(solution)/shard_map/ppermute | solution.py:19
where the time goes:
time: 76.6 us; the launch traced here: 76.1 us
  local copies, waits for them, and re-layouts  23 us (30%)
  starting transfers between devices  18.9 us (25%)
  waiting for transfers between devices  18.8 us (25%)
  loops' own time  8.5 us (11%)
  other arithmetic  5 us (7%)
  matrix products  1 us (1%)
  between operations  0.82 us (1%)
    all_to_all x1, waiting for transfers between devices, per_device(): lax.all_to_all(outgoing, 'xy', split_axis=0, concat_axis=0, tiled=True)  12.3 us
    gather x12, local copies, waits for them, and re-layouts  9.41 us
    another operation x1, loops' own time, spread_back(): return lax.fori_loop(0, smeared.shape[0], add_one, init)  8.41 us
    all_to_all x1, waiting for transfers between devices, per_device(): lax.all_to_all(returning, 'xy', split_axis=0, concat_axis=0, tiled=True)  5.2 us
    all_to_all x1, starting transfers between devices, per_device(): lax.all_to_all(out_rows, 'xy', split_axis=0, concat_axis=0, tiled=True)  5.17 us
    ppermute x1, starting transfers between devices, padded_2(): lax.ppermute(tail, axis, [(i, (i + 1) % count) for i in range(ends)])  4.58 us
    all_to_all x1, starting transfers between devices, per_device(): lax.all_to_all(outgoing, 'xy', split_axis=0, concat_axis=0, tiled=True)  4.23 us
    dynamic_update_slice x4, local copies, waits for them, and re-layouts, add_one(): update = lax.dynamic_update_slice_in_dim(update, piece, start, 1)  3.77 us
  transfers between devices with their start and end apart: 5, of which 3 were waited for; matrix products, arithmetic and copies ran while one was open for 18% of the time, Pallas kernels for 0%

commit v1 on v0

v1 whole, which is shorter than its diff:
```python
import functools

import jax
import jax.numpy as jnp
from jax import lax
from jax.experimental import pallas as pl
from jax.experimental.pallas import tpu as pltpu
from jax.sharding import PartitionSpec as P

relax = 1.0
tv_weight = 0.2
smooth_sq = 0.01

LANES = 128
TILE = 8
CHUNKS = 2
TERMS = 3


def bit_orders(bits, chunks):
    rest = list(range(1, bits))
    return [[0] + (rest if chunk % 2 == 0 else rest[::-1]) for chunk in range(chunks)]


def split_terms(x, terms):
    parts = []
    for _ in range(terms):
        part = x.astype(jnp.bfloat16)
        parts.append(part)
        x = x - part.astype(jnp.float32)
    return parts


def flip(index, bit):
    step = 1 << bit
    return index + step * (1 - 2 * ((index // step) % 2))


def sum_slabs(stacked, terms, rows):
    total = stacked[(terms - 1) * rows : terms * rows]
    for term in range(terms - 2, -1, -1):
        total = total + stacked[term * rows : (term + 1) * rows]
    return total


def rel_of(order, position):
    bits = len(order)
    return sum(((position >> (bits - 1 - j)) & 1) << bit for j, bit in enumerate(order))


def position_of(order, owner, me):
    bits = len(order)
    place = jnp.int32(0)
    for j, bit in enumerate(order):
        step = 1 << bit
        place = place + ((owner // step + me // step) % 2) * (1 << (bits - 1 - j))
    return place


def band(offsets, k, vxy, width):
    last_base = (vxy - width) // LANES - 1
    base = jnp.minimum(offsets[0, k] // LANES, last_base)
    return base * LANES, offsets[0, k] - base * LANES


def project_kernel(cfg, vol, mats, offsets, ray_lists, owner_map, *refs):
    count, bits, depth, vxy, width, rays, listed, chunks, gz_count = cfg
    rows = depth // chunks
    orders = bit_orders(bits, chunks)
    parts = refs[:chunks]
    found = refs[chunks]
    me = lax.axis_index("xy")
    span = width + LANES
    owners = [owner_map[ray_lists[me, k]] for k in range(listed)]
    ones = jnp.ones((16, width), jnp.bfloat16)
    found[listed] = jnp.zeros((depth + TILE, rays), jnp.float32)
    for k in range(listed):
        start, shift = band(offsets, k, vxy, width)
        window = vol[:, pl.ds(pl.multiple_of(start, LANES), span)]
        window = pltpu.roll(window, span - shift, 1)[:, :width]
        lhs = jnp.concatenate(split_terms(window, TERMS) + [ones], axis=0)
        product = jnp.dot(lhs, mats[0, k], preferred_element_type=jnp.float32)
        found[k, :depth] = sum_slabs(product, TERMS, depth)
        found[k, depth:] = product[TERMS * depth : TERMS * depth + TILE]
    for position in range(count):
        for chunk in range(chunks):
            rel = rel_of(orders[chunk], position)
            owner = me
            for bit in range(bits):
                if (rel >> bit) & 1:
                    owner = flip(owner, bit)
            slot = jnp.int32(listed)
            for k in range(listed):
                slot = jnp.where(owners[k] == owner, jnp.int32(k), slot)
            top = chunk * rows
            parts[chunk][position, :rows] = found[slot, top : top + rows]
            if chunk == 0:
                parts[chunk][position, rows:] = found[slot, depth:]


def exchange_kernel(cfg, vol, sino, mats, *refs):
    count, bits, depth, vxy, width, rays, listed, chunks, gz_count = cfg
    rows = depth // chunks
    half = count // 2
    orders = bit_orders(bits, chunks)
    refs = list(refs)

    def take(number):
        taken = refs[:number]
        del refs[:number]
        return taken

    parts = take(chunks)
    ray_values = take(chunks)
    terms, smoothed = take(2)
    sums = take(chunks)
    landed = take(chunks)
    padded, send_sem, recv_sem, halo_send, halo_recv = refs

    me = lax.axis_index("xy")
    slab = lax.axis_index("gz")
    partners = [flip(me, bit) for bit in range(bits)]

    barrier = pltpu.get_barrier_semaphore()
    for partner in partners:
        pl.semaphore_signal(barrier, inc=1, device_id={"xy": partner}, device_id_type=pl.DeviceIdType.MESH)

    @pl.when(slab > 0)
    def _():
        pl.semaphore_signal(barrier, inc=1, device_id={"gz": slab - 1}, device_id_type=pl.DeviceIdType.MESH)

    @pl.when(slab < gz_count - 1)
    def _():
        pl.semaphore_signal(barrier, inc=1, device_id={"gz": slab + 1}, device_id_type=pl.DeviceIdType.MESH)

    has_below = (slab > 0).astype(jnp.int32)
    has_above = (slab < gz_count - 1).astype(jnp.int32)
    pl.semaphore_wait(barrier, bits + has_below + has_above)

    def remote(src, dst, chunk, number, partner):
        return pltpu.make_async_remote_copy(
            src_ref=src,
            dst_ref=dst,
            send_sem=send_sem.at[chunk, number],
            recv_sem=recv_sem.at[chunk, number],
            device_id={"xy": partner},
            device_id_type=pl.DeviceIdType.MESH,
        )

    pending = []
    live = {}

    def reduce_send(chunk, stage):
        low = half >> stage
        source = parts[chunk] if stage == 0 else sums[chunk]
        copy = remote(
            source.at[pl.ds(low, low)],
            landed[chunk].at[pl.ds(low, low)],
            chunk,
            stage,
            partners[orders[chunk][stage]],
        )
        copy.start()
        live[chunk] = copy
        pending.append(copy)

    def add_landed(chunk, stage, positions):
        low = half >> stage
        source = parts[chunk] if stage == 0 else sums[chunk]
        for position in positions:
            sums[chunk][position] = source[position] + landed[chunk][low + position]

    def gather_send(chunk, stage):
        held = count >> (stage + 1)
        copy = remote(
            ray_values[chunk].at[pl.ds(0, held)],
            ray_values[chunk].at[pl.ds(held, held)],
            chunk,
            bits + stage,
            partners[orders[chunk][stage]],
        )
        copy.start()
        live[chunk] = copy
        pending.append(copy)

    def halo_up():
        return pltpu.make_async_remote_copy(
            src_ref=vol.at[pl.ds(depth - TILE, TILE)],
            dst_ref=padded.at[pl.ds(0, TILE)],
            send_sem=halo_send.at[0],
            recv_sem=halo_recv.at[0],
            device_id={"gz": slab + 1},
            device_id_type=pl.DeviceIdType.MESH,
        )

    def halo_down():
        return pltpu.make_async_remote_copy(
            src_ref=vol.at[pl.ds(0, TILE)],
            dst_ref=padded.at[pl.ds(TILE + depth, TILE)],
            send_sem=halo_send.at[1],
            recv_sem=halo_recv.at[1],
            device_id={"gz": slab - 1},
            device_id_type=pl.DeviceIdType.MESH,
        )

    for chunk in range(chunks):
        reduce_send(chunk, 0)

    @pl.when(slab < gz_count - 1)
    def _():
        halo_up().start()

    @pl.when(slab > 0)
    def _():
        halo_down().start()

    for stage in range(1, bits):
        for chunk in range(chunks):
            live[chunk].wait_recv()
            low = half >> stage
            add_landed(chunk, stage - 1, range(low, 2 * low))
            reduce_send(chunk, stage)
            add_landed(chunk, stage - 1, range(low))

        if stage == 1:
            ones = jnp.ones((16, rays), jnp.bfloat16)
            for k in range(listed):
                terms[k] = lax.dot_general(
                    ones, mats[0, k], (((1,), (1,)), ((), ())), preferred_element_type=jnp.float32
                )[:TILE]
            padded[TILE : TILE + depth, :] = vol[...]

            @pl.when(slab == 0)
            def _():
                padded[:TILE, :] = jnp.zeros((TILE, vxy), jnp.float32)

            @pl.when(slab == gz_count - 1)
            def _():
                padded[TILE + depth :, :] = jnp.zeros((TILE, vxy), jnp.float32)

    def smooth():
        @pl.when(slab > 0)
        def _():
            halo_up().wait_recv()

        @pl.when(slab < gz_count - 1)
        def _():
            halo_down().wait_recv()

        for lane in range(0, vxy, LANES):
            lanes = slice(lane, lane + LANES)
            diffs = padded[TILE : TILE + depth + 1, lanes] - padded[TILE - 1 : TILE + depth, lanes]
            slopes = diffs * lax.rsqrt(diffs * diffs + smooth_sq)
            smoothed[:, lanes] = vol[:, lanes] - tv_weight * (slopes[:depth] - slopes[1:])

    smooth()
    rowsum = None
    for chunk in range(chunks):
        live[chunk].wait_recv()
        add_landed(chunk, bits - 1, [0])
        total = sums[chunk][0]
        if chunk == 0:
            rowsum = total[rows : rows + 1]
        top = chunk * rows
        ray_values[chunk][0] = (sino[top : top + rows, :] - total[:rows]) / rowsum
        gather_send(chunk, bits - 1)
    for stage in range(bits - 2, -1, -1):
        for chunk in range(chunks):
            live[chunk].wait_recv()
            gather_send(chunk, stage)
    for chunk in range(chunks):
        live[chunk].wait_recv()
    for copy in pending:
        copy.wait_send()

    @pl.when(slab < gz_count - 1)
    def _():
        halo_up().wait_send()

    @pl.when(slab > 0)
    def _():
        halo_down().wait_send()


def back_kernel(cfg, smoothed, terms, mats, offsets, ray_lists, owner_map, *refs):
    count, bits, depth, vxy, width, rays, listed, chunks, gz_count = cfg
    rows = depth // chunks
    orders = bit_orders(bits, chunks)
    ray_values = refs[:chunks]
    new_vol, weighted_out, spread = refs[chunks:]
    me = lax.axis_index("xy")
    span = width + LANES
    margin = vxy - span
    high = depth + TILE
    for chunk in range(chunks):
        weighted_out[chunk * rows : (chunk + 1) * rows, :] = ray_values[chunk][0]
    spread[:, :, :margin] = jnp.zeros((listed, high, margin), jnp.float32)
    spread[:, :, margin + span :] = jnp.zeros((listed, high, margin), jnp.float32)
    places = []
    for k in range(listed):
        owner = owner_map[ray_lists[me, k]]
        needed = jnp.concatenate(
            [ray_values[c][position_of(orders[c], owner, me)] for c in range(chunks)], axis=0
        )
        stacked = lax.dot_general(
            jnp.concatenate(split_terms(needed, TERMS), axis=0),
            mats[0, k],
            (((1,), (1,)), ((), ())),
            preferred_element_type=jnp.float32,
        )
        start, shift = band(offsets, k, vxy, width)
        piece = jnp.concatenate([sum_slabs(stacked, TERMS, depth), terms[k]], axis=0)
        wide = jnp.concatenate([piece, jnp.zeros((high, LANES), jnp.float32)], axis=1)
        spread[k, :, margin : margin + span] = pltpu.roll(wide, shift, 1)
        places.append(margin - start)
    for lane in range(0, vxy, LANES):
        total = None
        for k in range(listed):
            piece = spread[k, :, pl.ds(pl.multiple_of(places[k] + lane, LANES), LANES)]
            total = piece if total is None else total + piece
        lanes = slice(lane, lane + LANES)
        scale = relax / jnp.maximum(total[depth : depth + 1], 1.0)
        new_vol[:, lanes] = smoothed[:, lanes] + total[:depth] * scale


def per_device(cfg, volume, sinogram, ray_mats, offsets, ray_lists, owner_map):
    count, bits, depth, vxy, width, rays, listed, chunks, gz_count = cfg
    rows = depth // chunks
    high = [rows + (TILE if chunk == 0 else 0) for chunk in range(chunks)]
    f32 = jnp.float32
    vmem = pl.BlockSpec(memory_space=pltpu.VMEM)
    smem = pl.BlockSpec(memory_space=pltpu.SMEM)
    limit = 24 * 1024 * 1024

    def shape(*dims):
        return jax.ShapeDtypeStruct(dims, f32)

    parts = pl.pallas_call(
        functools.partial(project_kernel, cfg),
        out_shape=tuple(shape(count, h, rays) for h in high),
        in_specs=[vmem, vmem, smem, smem, smem],
        out_specs=(vmem,) * chunks,
        scratch_shapes=[pltpu.VMEM((listed + 1, depth + TILE, rays), f32)],
        compiler_params=pltpu.CompilerParams(vmem_limit_bytes=limit),
    )(volume, ray_mats, offsets, ray_lists, owner_map)

    *ray_values, terms, smoothed = pl.pallas_call(
        functools.partial(exchange_kernel, cfg),
        out_shape=tuple(shape(count, rows, rays) for _ in range(chunks))
        + (shape(listed, TILE, width), shape(depth, vxy)),
        in_specs=[vmem] * (3 + chunks),
        out_specs=(vmem,) * (chunks + 2),
        scratch_shapes=[pltpu.VMEM((count // 2, h, rays), f32) for h in high]
        + [pltpu.VMEM((count, h, rays), f32) for h in high]
        + [
            pltpu.VMEM((depth + 2 * TILE, vxy), f32),
            pltpu.SemaphoreType.DMA((chunks, 2 * bits)),
            pltpu.SemaphoreType.DMA((chunks, 2 * bits)),
            pltpu.SemaphoreType.DMA((2,)),
            pltpu.SemaphoreType.DMA((2,)),
        ],
        compiler_params=pltpu.CompilerParams(
            collective_id=0, has_side_effects=True, vmem_limit_bytes=limit
        ),
    )(volume, sinogram, ray_mats, *parts)

    return pl.pallas_call(
        functools.partial(back_kernel, cfg),
        out_shape=(shape(depth, vxy), shape(depth, rays)),
        in_specs=[vmem] * 3 + [smem] * 3 + [vmem] * chunks,
        out_specs=(vmem, vmem),
        scratch_shapes=[pltpu.VMEM((listed, depth + TILE, 2 * vxy - width - LANES), f32)],
        compiler_params=pltpu.CompilerParams(vmem_limit_bytes=limit),
    )(smoothed, terms, ray_mats, offsets, ray_lists, owner_map, *ray_values)


def solution(mesh):
    in_specs = (P("gz", "xy"), P("gz", "xy"), P("xy", None, None, None), P("xy", None), P(), P())
    out_specs = (P("gz", "xy"), P("gz", "xy"))
    count = mesh.shape["xy"]
    gz_count = mesh.shape["gz"]

    def whole(volume, sinogram, ray_mats, offsets, ray_lists, owner_map):
        cfg = (
            count,
            count.bit_length() - 1,
            volume.shape[0] // gz_count,
            volume.shape[1] // count,
            ray_mats.shape[2],
            ray_mats.shape[3],
            ray_mats.shape[1],
            CHUNKS,
            gz_count,
        )
        return jax.shard_map(
            functools.partial(per_device, cfg),
            mesh=mesh,
            in_specs=in_specs,
            out_specs=out_specs,
            check_vma=False,
        )(volume, sinogram, ray_mats, offsets, ray_lists, owner_map)

    return whole
```

time: 76.6 us -> 27.6 us (0.36)
  Pallas kernels: 0 us -> 23.9 us
  local copies, waits for them, and re-layouts: 23 us -> 2.82 us
  starting transfers between devices: 18.9 us -> 0 us
  waiting for transfers between devices: 18.8 us -> 0 us
  loops' own time: 8.5 us -> 0 us
  other arithmetic: 5 us -> 0 us
  matrix products: 1 us -> 0 us
    pallas_call x0 -> x3, Pallas kernels: none -> 23.9 us  [the longest x1 20.6 us: per_device(): pl.pallas_call(functools.partial(exchange_kernel, cfg), out_shape=tuple((...]
    all_to_all x3 -> x0, waiting for transfers between devices: 17.5 us -> none  [the longest x1 12.3 us: per_device(): lax.all_to_all(outgoing, 'xy', split_axis=0, concat_axis=0, tiled=True)]
    all_to_all x3 -> x0, starting transfers between devices: 13.1 us -> none  [the longest x1 5.17 us: per_device(): lax.all_to_all(out_rows, 'xy', split_axis=0, concat_axis=0, tiled=True)]
    gather x13 -> x0, local copies, waits for them, and re-layouts: 9.98 us -> none
    another operation x2 -> x0, loops' own time: 8.5 us -> none  [the longest x1 8.41 us: spread_back(): return lax.fori_loop(0, smeared.shape[0], add_one, init)]
    ppermute x2 -> x0, starting transfers between devices: 5.87 us -> none  [the longest x1 4.58 us: padded_2(): lax.ppermute(tail, axis, [(i, (i + 1) % count) for i in range(ends)])]
    dynamic_update_slice x4 -> x0, local copies, waits for them, and re-layouts: 3.77 us -> none  [add_one(): update = lax.dynamic_update_slice_in_dim(update, piece, start, 1)]
    scatter x3 -> x0, local copies, waits for them, and re-layouts: 3.55 us -> none  [the longest x1 2.34 us: per_device(): jnp.zeros((count,) + partial_value.shape[1:], jnp.float32).at[owners]]
  transfers between devices with their start and end apart: 5 -> 0, of which waited for: 3 -> 0; matrix products, arithmetic and copies ran while one was open for 18% -> 0% of each run, Pallas kernels for 0% -> 0%
where the time goes in v1:
time: 27.6 us; the launch traced here: 27.4 us
  Pallas kernels  23.9 us (87%)
  local copies, waits for them, and re-layouts  2.82 us (10%)
  between operations  0.69 us (2%)
    pallas_call x1, Pallas kernels, per_device(): pl.pallas_call(functools.partial(exchange_kernel, cfg), out_shape=tuple((...  20.6 us
    unnamed x13, local copies, waits for them, and re-layouts  2.82 us
    pallas_call x1, Pallas kernels, per_device(): pl.pallas_call(functools.partial(back_kernel, cfg), out_shape=(shape(dept...  2.14 us
    pallas_call x1, Pallas kernels, per_device(): pl.pallas_call(functools.partial(project_kernel, cfg), out_shape=tuple((s...  1.12 us

profile of v1, /device:TPU:0, one launch (start us, length us, event | category | flops | bytes accessed | tf_op | source)
XLA Modules:
  0.0 27.4 jit_solution(1325930197063189092)
XLA Ops:
  0.6 0.0 copy-start.5
  0.6 0.0 copy-start.4
  0.7 0.8 %copy.8.ray_lists = s32[8,4]{1,0:T(8,128)S(1)} copy(s32[8,4]{0,1:T(4,128)} %param.10) | data formatting | bytes 256 | tf_op args[4]
  1.4 0.0 copy-done.5
  1.4 0.0 copy-done.4
  1.4 0.0 copy-start
  1.4 1.0 %copy-done = bf16[1,4,256,256]{3,2,1,0:T(8,128)(2,1)S(1)} copy-done((bf16[1,4,256,256]{3,2,1,0:T(8,128)(2,1)S(1)}, bf16[1,4,256,256]{3,2,1,0:T(8,128)(2,1)}, u32[]{:S(2)}) %copy-start) | copy-done | bytes 524312
  2.5 0.0 copy-start.2
  2.5 1.0 %copy-done.2 = f32[96,1024]{1,0:T(8,128)S(1)} copy-done((f32[96,1024]{1,0:T(8,128)S(1)}, f32[96,1024]{1,0:T(8,128)}, u32[]{:S(2)}) %copy-start.2) | copy-done | bytes 393240
  3.5 0.0 copy-start.3
  3.5 1.1 %shard_map.77 = (f32[8,56,256]{2,1,0:T(8,128)S(1)}, f32[8,48,256]{2,1,0:T(8,128)S(1)}) custom-call(f32[96,1024]{1,0:T(8,128)S(1)} %copy-done.2, bf16[1,4,256,256]{3,2,1,0:T(8,128)(2,1)S(1)} %copy-done, s32[1,4]{1,0:T(1,128)S(1)} %copy-done.4, s32[8,4]{1,0:T(8,128)S(1)} %copy.8.ray_lists, s32[8]{0:T(128)S(1)} %copy-done.5), custom_call_target="tpu_custom_call" | custom-call | tf_op jit(solution)/shard_map/pallas_call | solution.py:338
  4.6 0.0 copy-done.3
  4.6 0.0 copy-start.1
  4.6 20.6 %shard_map.78 = (f32[8,48,256]{2,1,0:T(8,128)S(1)}, f32[8,48,256]{2,1,0:T(8,128)S(1)}, f32[4,8,256]{2,1,0:T(8,128)S(1)}, f32[96,1024]{1,0:T(8,128)S(1)}) custom-call(f32[96,1024]{1,0:T(8,128)S(1)} %copy-done.2, f32[96,256]{1,0:T(8,128)S(1)} %copy-done.3, bf16[1,4,256,256]{3,2,1,0:T(8,128)(2,1)S(1)} %copy-done, f32[8,56,256]{2,1,0:T(8,128)S(1)} %get-tuple-element.8.refs_0_, ...), custom_call_target="tpu_custom_call" | custom-call | tf_op jit(solution)/shard_map/pallas_call | solution.py:347
  25.2 0.0 copy-done.1
  25.2 2.1 %shard_map.79 = (f32[96,1024]{1,0:T(8,128)}, f32[96,256]{1,0:T(8,128)}) custom-call(f32[96,1024]{1,0:T(8,128)S(1)} %get-tuple-element.10.smoothed, f32[4,8,256]{2,1,0:T(8,128)S(1)} %get-tuple-element.11.terms, bf16[1,4,256,256]{3,2,1,0:T(8,128)(2,1)S(1)} %copy-done.1, s32[1,4]{1,0:T(1,128)S(1)} %copy-done.4, s32[8,4]{1,0:T(8,128)S(1)} %copy.8.ray_lists, ...), custom_call_target="tpu_custom_call" | custom-call | tf_op jit(solution)/shard_map/pallas_call | solution.py:367
Async XLA Ops:
  0.6 0.8 %copy-start.5 = (s32[8]{0:T(128)S(1)}, s32[8]{0:T(128)}, u32[]{:S(2)}) copy-start(s32[8]{0:T(128)} %owner_map.3) | copy-start | bytes 100
  0.6 0.8 %copy-start.4 = (s32[1,4]{1,0:T(1,128)S(1)}, s32[1,4]{1,0:T(1,128)}, u32[]{:S(2)}) copy-start(s32[1,4]{1,0:T(1,128)} %offsets.3) | copy-start | bytes 52
  1.4 1.0 %copy-start = (bf16[1,4,256,256]{3,2,1,0:T(8,128)(2,1)S(1)}, bf16[1,4,256,256]{3,2,1,0:T(8,128)(2,1)}, u32[]{:S(2)}) copy-start(bf16[1,4,256,256]{3,2,1,0:T(8,128)(2,1)} %mats.5) | copy-start | bytes 1572868
  2.5 1.0 %copy-start.2 = (f32[96,1024]{1,0:T(8,128)S(1)}, f32[96,1024]{1,0:T(8,128)}, u32[]{:S(2)}) copy-start(f32[96,1024]{1,0:T(8,128)} %vol.3) | copy-start | bytes 1179652
  3.5 1.1 %copy-start.3 = (f32[96,256]{1,0:T(8,128)S(1)}, f32[96,256]{1,0:T(8,128)}, u32[]{:S(2)}) copy-start(f32[96,256]{1,0:T(8,128)} %sino.1) | copy-start | bytes 294916
  4.6 20.6 %copy-start.1 = (bf16[1,4,256,256]{3,2,1,0:T(8,128)(2,1)S(1)}, bf16[1,4,256,256]{3,2,1,0:T(8,128)(2,1)}, u32[]{:S(2)}) copy-start(bf16[1,4,256,256]{3,2,1,0:T(8,128)(2,1)} %mats.5) | copy-start | bytes 1572868

commit v2 on v1

--- a/solution.py
+++ b/solution.py
@@ -13,13 +13,8 @@
 
 LANES = 128
 TILE = 8
-CHUNKS = 2
+CHUNKS = 3
 TERMS = 3
-
-
-def bit_orders(bits, chunks):
-    rest = list(range(1, bits))
-    return [[0] + (rest if chunk % 2 == 0 else rest[::-1]) for chunk in range(chunks)]
 
 
 def split_terms(x, terms):
@@ -43,17 +38,19 @@
     return total
 
 
-def rel_of(order, position):
-    bits = len(order)
-    return sum(((position >> (bits - 1 - j)) & 1) << bit for j, bit in enumerate(order))
-
-
-def position_of(order, owner, me):
-    bits = len(order)
-    place = jnp.int32(0)
-    for j, bit in enumerate(order):
+def partner_at(me, position, bits):
+    other = flip(me, 0) if (position >> (bits - 1)) & 1 else me
+    for bit in range(1, bits):
+        if (position >> (bit - 1)) & 1:
+            other = flip(other, bit)
+    return other
+
+
+def position_of(owner, me, bits):
+    place = ((owner + me) % 2) * (1 << (bits - 1))
+    for bit in range(1, bits):
         step = 1 << bit
-        place = place + ((owner // step + me // step) % 2) * (1 << (bits - 1 - j))
+        place = place + ((owner // step + me // step) % 2) * (1 << (bit - 1))
     return place
 
 
@@ -63,15 +60,14 @@
     return base * LANES, offsets[0, k] - base * LANES
 
 
-def project_kernel(cfg, vol, mats, offsets, ray_lists, owner_map, *refs):
+def project_kernel(cfg, vol, mats, offsets, lists, owner_map, *refs):
     count, bits, depth, vxy, width, rays, listed, chunks, gz_count = cfg
     rows = depth // chunks
-    orders = bit_orders(bits, chunks)
     parts = refs[:chunks]
     found = refs[chunks]
     me = lax.axis_index("xy")
     span = width + LANES
-    owners = [owner_map[ray_lists[me, k]] for k in range(listed)]
+    owners = [owner_map[lists[k, me]] for k in range(listed)]
     ones = jnp.ones((16, width), jnp.bfloat16)
     found[listed] = jnp.zeros((depth + TILE, rays), jnp.float32)
     for k in range(listed):
@@ -83,15 +79,11 @@
         found[k, :depth] = sum_slabs(product, TERMS, depth)
         found[k, depth:] = product[TERMS * depth : TERMS * depth + TILE]
     for position in range(count):
+        owner = partner_at(me, position, bits)
+        slot = jnp.int32(listed)
+        for k in range(listed):
+            slot = jnp.where(owners[k] == owner, jnp.int32(k), slot)
         for chunk in range(chunks):
-            rel = rel_of(orders[chunk], position)
-            owner = me
-            for bit in range(bits):
-                if (rel >> bit) & 1:
-                    owner = flip(owner, bit)
-            slot = jnp.int32(listed)
-            for k in range(listed):
-                slot = jnp.where(owners[k] == owner, jnp.int32(k), slot)
             top = chunk * rows
             parts[chunk][position, :rows] = found[slot, top : top + rows]
             if chunk == 0:
@@ -102,7 +94,6 @@
     count, bits, depth, vxy, width, rays, listed, chunks, gz_count = cfg
     rows = depth // chunks
     half = count // 2
-    orders = bit_orders(bits, chunks)
     refs = list(refs)
 
     def take(number):
@@ -119,7 +110,9 @@
 
     me = lax.axis_index("xy")
     slab = lax.axis_index("gz")
-    partners = [flip(me, bit) for bit in range(bits)]
+    sibling = flip(me, 0)
+    direct = list(range(half - 1, 0, -1))
+    partners = [sibling] + [partner_at(me, p, bits) for p in range(1, half)]
 
     barrier = pltpu.get_barrier_semaphore()
     for partner in partners:
@@ -135,7 +128,7 @@
 
     has_below = (slab > 0).astype(jnp.int32)
     has_above = (slab < gz_count - 1).astype(jnp.int32)
-    pl.semaphore_wait(barrier, bits + has_below + has_above)
+    pl.semaphore_wait(barrier, half + has_below + has_above)
 
     def remote(src, dst, chunk, number, partner):
         return pltpu.make_async_remote_copy(
@@ -147,41 +140,21 @@
             device_id_type=pl.DeviceIdType.MESH,
         )
 
-    pending = []
-    live = {}
-
-    def reduce_send(chunk, stage):
-        low = half >> stage
-        source = parts[chunk] if stage == 0 else sums[chunk]
-        copy = remote(
-            source.at[pl.ds(low, low)],
-            landed[chunk].at[pl.ds(low, low)],
-            chunk,
-            stage,
-            partners[orders[chunk][stage]],
-        )
-        copy.start()
-        live[chunk] = copy
-        pending.append(copy)
-
-    def add_landed(chunk, stage, positions):
-        low = half >> stage
-        source = parts[chunk] if stage == 0 else sums[chunk]
-        for position in positions:
-            sums[chunk][position] = source[position] + landed[chunk][low + position]
-
-    def gather_send(chunk, stage):
-        held = count >> (stage + 1)
-        copy = remote(
-            ray_values[chunk].at[pl.ds(0, held)],
-            ray_values[chunk].at[pl.ds(held, held)],
-            chunk,
-            bits + stage,
-            partners[orders[chunk][stage]],
-        )
-        copy.start()
-        live[chunk] = copy
-        pending.append(copy)
+    def sibling_parts(chunk):
+        return remote(
+            parts[chunk].at[pl.ds(half, half)], landed[chunk].at[pl.ds(half, half)], chunk, 0, sibling
+        )
+
+    def reduce_copy(chunk, p):
+        return remote(sums[chunk].at[p], landed[chunk].at[p], chunk, p, partners[p])
+
+    def gather_copy(chunk, p):
+        return remote(ray_values[chunk].at[0], ray_values[chunk].at[p], chunk, half + p, partners[p])
+
+    def relay_copy(chunk, p):
+        return remote(
+            ray_values[chunk].at[p], ray_values[chunk].at[half + p], chunk, 2 * half + p, sibling
+        )
 
     def halo_up():
         return pltpu.make_async_remote_copy(
@@ -204,7 +177,7 @@
         )
 
     for chunk in range(chunks):
-        reduce_send(chunk, 0)
+        sibling_parts(chunk).start()
 
     @pl.when(slab < gz_count - 1)
     def _():
@@ -214,29 +187,27 @@
     def _():
         halo_down().start()
 
-    for stage in range(1, bits):
-        for chunk in range(chunks):
-            live[chunk].wait_recv()
-            low = half >> stage
-            add_landed(chunk, stage - 1, range(low, 2 * low))
-            reduce_send(chunk, stage)
-            add_landed(chunk, stage - 1, range(low))
-
-        if stage == 1:
-            ones = jnp.ones((16, rays), jnp.bfloat16)
-            for k in range(listed):
-                terms[k] = lax.dot_general(
-                    ones, mats[0, k], (((1,), (1,)), ((), ())), preferred_element_type=jnp.float32
-                )[:TILE]
-            padded[TILE : TILE + depth, :] = vol[...]
-
-            @pl.when(slab == 0)
-            def _():
-                padded[:TILE, :] = jnp.zeros((TILE, vxy), jnp.float32)
-
-            @pl.when(slab == gz_count - 1)
-            def _():
-                padded[TILE + depth :, :] = jnp.zeros((TILE, vxy), jnp.float32)
+    for chunk in range(chunks):
+        sibling_parts(chunk).wait_recv()
+        for p in direct:
+            sums[chunk][p] = parts[chunk][p] + landed[chunk][half + p]
+            reduce_copy(chunk, p).start()
+        sums[chunk][0] = parts[chunk][0] + landed[chunk][half]
+
+    ones = jnp.ones((16, rays), jnp.bfloat16)
+    for k in range(listed):
+        terms[k] = lax.dot_general(
+            ones, mats[0, k], (((1,), (1,)), ((), ())), preferred_element_type=jnp.float32
+        )[:TILE]
+    padded[TILE : TILE + depth, :] = vol[...]
+
+    @pl.when(slab == 0)
+    def _():
+        padded[:TILE, :] = jnp.zeros((TILE, vxy), jnp.float32)
+
+    @pl.when(slab == gz_count - 1)
+    def _():
+        padded[TILE + depth :, :] = jnp.zeros((TILE, vxy), jnp.float32)
 
     def smooth():
         @pl.when(slab > 0)
@@ -256,22 +227,31 @@
     smooth()
     rowsum = None
     for chunk in range(chunks):
-        live[chunk].wait_recv()
-        add_landed(chunk, bits - 1, [0])
         total = sums[chunk][0]
+        for p in range(1, half):
+            reduce_copy(chunk, p).wait_recv()
+            total = total + landed[chunk][p]
         if chunk == 0:
             rowsum = total[rows : rows + 1]
         top = chunk * rows
         ray_values[chunk][0] = (sino[top : top + rows, :] - total[:rows]) / rowsum
-        gather_send(chunk, bits - 1)
-    for stage in range(bits - 2, -1, -1):
-        for chunk in range(chunks):
-            live[chunk].wait_recv()
-            gather_send(chunk, stage)
-    for chunk in range(chunks):
-        live[chunk].wait_recv()
-    for copy in pending:
-        copy.wait_send()
+        for p in direct:
+            gather_copy(chunk, p).start()
+        relay_copy(chunk, 0).start()
+    for chunk in range(chunks):
+        for p in range(1, half):
+            gather_copy(chunk, p).wait_recv()
+            relay_copy(chunk, p).start()
+    for chunk in range(chunks):
+        for p in range(half):
+            relay_copy(chunk, p).wait_recv()
+    for chunk in range(chunks):
+        sibling_parts(chunk).wait_send()
+        for p in range(half):
+            if p:
+                reduce_copy(chunk, p).wait_send()
+                gather_copy(chunk, p).wait_send()
+            relay_copy(chunk, p).wait_send()
 
     @pl.when(slab < gz_count - 1)
     def _():
@@ -282,10 +262,9 @@
         halo_down().wait_send()
 
 
-def back_kernel(cfg, smoothed, terms, mats, offsets, ray_lists, owner_map, *refs):
+def back_kernel(cfg, smoothed, terms, mats, offsets, lists, owner_map, *refs):
     count, bits, depth, vxy, width, rays, listed, chunks, gz_count = cfg
     rows = depth // chunks
-    orders = bit_orders(bits, chunks)
     ray_values = refs[:chunks]
     new_vol, weighted_out, spread = refs[chunks:]
     me = lax.axis_index("xy")
@@ -298,10 +277,8 @@
     spread[:, :, margin + span :] = jnp.zeros((listed, high, margin), jnp.float32)
     places = []
     for k in range(listed):
-        owner = owner_map[ray_lists[me, k]]
-        needed = jnp.concatenate(
-            [ray_values[c][position_of(orders[c], owner, me)] for c in range(chunks)], axis=0
-        )
+        place = position_of(owner_map[lists[k, me]], me, bits)
+        needed = jnp.concatenate([ray_values[c][place] for c in range(chunks)], axis=0)
         stacked = lax.dot_general(
             jnp.concatenate(split_terms(needed, TERMS), axis=0),
             mats[0, k],
@@ -335,6 +312,7 @@
     def shape(*dims):
         return jax.ShapeDtypeStruct(dims, f32)
 
+    lists = ray_lists.T
     parts = pl.pallas_call(
         functools.partial(project_kernel, cfg),
         out_shape=tuple(shape(count, h, rays) for h in high),
@@ -342,7 +320,7 @@
         out_specs=(vmem,) * chunks,
         scratch_shapes=[pltpu.VMEM((listed + 1, depth + TILE, rays), f32)],
         compiler_params=pltpu.CompilerParams(vmem_limit_bytes=limit),
-    )(volume, ray_mats, offsets, ray_lists, owner_map)
+    )(volume, ray_mats, offsets, lists, owner_map)
 
     *ray_values, terms, smoothed = pl.pallas_call(
         functools.partial(exchange_kernel, cfg),
@@ -354,8 +332,8 @@
         + [pltpu.VMEM((count, h, rays), f32) for h in high]
         + [
             pltpu.VMEM((depth + 2 * TILE, vxy), f32),
-            pltpu.SemaphoreType.DMA((chunks, 2 * bits)),
-            pltpu.SemaphoreType.DMA((chunks, 2 * bits)),
+            pltpu.SemaphoreType.DMA((chunks, 3 * count // 2)),
+            pltpu.SemaphoreType.DMA((chunks, 3 * count // 2)),
             pltpu.SemaphoreType.DMA((2,)),
             pltpu.SemaphoreType.DMA((2,)),
         ],
@@ -371,7 +349,7 @@
         out_specs=(vmem, vmem),
         scratch_shapes=[pltpu.VMEM((listed, depth + TILE, 2 * vxy - width - LANES), f32)],
         compiler_params=pltpu.CompilerParams(vmem_limit_bytes=limit),
-    )(smoothed, terms, ray_mats, offsets, ray_lists, owner_map, *ray_values)
+    )(smoothed, terms, ray_mats, offsets, lists, owner_map, *ray_values)
 
 
 def solution(mesh):

time: 27.6 us -> 24.6 us (0.89)
  Pallas kernels: 23.9 us -> 20.3 us
  local copies, waits for them, and re-layouts: 2.82 us -> 3.38 us
    pallas_call x1, Pallas kernels: 20.6 us -> 17.1 us  [per_device(): pl.pallas_call(functools.partial(exchange_kernel, cfg), out_shape=tuple((...]
    unnamed x13 -> x14, local copies, waits for them, and re-layouts: 2.82 us -> 3.38 us
where the time goes in v2:
time: 24.6 us; the launch traced here: 24.4 us
  Pallas kernels  20.3 us (83%)
  local copies, waits for them, and re-layouts  3.38 us (14%)
  between operations  0.69 us (3%)
    pallas_call x1, Pallas kernels, per_device(): pl.pallas_call(functools.partial(exchange_kernel, cfg), out_shape=tuple((...  17.1 us
    unnamed x14, local copies, waits for them, and re-layouts  3.38 us
    pallas_call x1, Pallas kernels, per_device(): pl.pallas_call(functools.partial(back_kernel, cfg), out_shape=(shape(dept...  2.11 us
    pallas_call x1, Pallas kernels, per_device(): pl.pallas_call(functools.partial(project_kernel, cfg), out_shape=tuple((s...  1.09 us

profile of v2, /device:TPU:0, one launch (start us, length us, event | category | flops | bytes accessed | tf_op | source)
XLA Modules:
  0.0 24.4 jit_solution(4423027757736756571)
XLA Ops:
  0.6 0.0 copy-start.6
  0.6 0.0 copy-start.5
  0.7 0.6 %copy-done.6 = s32[8]{0:T(128)S(1)} copy-done((s32[8]{0:T(128)S(1)}, s32[8]{0:T(128)}, u32[]{:S(2)}) %copy-start.6) | copy-done | bytes 56
  1.3 0.0 copy-done.5
  1.3 0.0 copy-start
  1.3 1.0 %copy-done = bf16[1,4,256,256]{3,2,1,0:T(8,128)(2,1)S(1)} copy-done((bf16[1,4,256,256]{3,2,1,0:T(8,128)(2,1)S(1)}, bf16[1,4,256,256]{3,2,1,0:T(8,128)(2,1)}, u32[]{:S(2)}) %copy-start) | copy-done | bytes 524312
  2.3 0.0 copy-start.2
  2.3 1.0 %copy-done.2 = f32[96,1024]{1,0:T(8,128)S(1)} copy-done((f32[96,1024]{1,0:T(8,128)S(1)}, f32[96,1024]{1,0:T(8,128)}, u32[]{:S(2)}) %copy-start.2) | copy-done | bytes 393240
  3.3 0.0 copy-start.4
  3.3 0.7 %copy-done.4 = s32[8,4]{0,1:T(4,128)S(1)} copy-done((s32[8,4]{0,1:T(4,128)S(1)}, s32[8,4]{0,1:T(4,128)}, u32[]{:S(2)}) %copy-start.4) | copy-done | bytes 152
  4.0 0.0 copy-start.3
  4.0 1.1 %shard_map.77 = (f32[8,40,256]{2,1,0:T(8,128)S(1)}, f32[8,32,256]{2,1,0:T(8,128)S(1)}, f32[8,32,256]{2,1,0:T(8,128)S(1)}) custom-call(f32[96,1024]{1,0:T(8,128)S(1)} %copy-done.2, bf16[1,4,256,256]{3,2,1,0:T(8,128)(2,1)S(1)} %copy-done, s32[1,4]{1,0:T(1,128)S(1)} %copy-done.5, s32[4,8]{1,0:T(4,128)S(1)} %bitcast.1, s32[8]{0:T(128)S(1)} %copy-done.6), custom_call_target="tpu_custom_call" | custom-call | tf_op jit(solution)/shard_map/pallas_call | solution.py:316
  5.1 0.0 copy-done.3
  5.1 0.0 copy-start.1
  5.1 17.1 %shard_map.78 = (f32[8,32,256]{2,1,0:T(8,128)S(1)}, f32[8,32,256]{2,1,0:T(8,128)S(1)}, f32[8,32,256]{2,1,0:T(8,128)S(1)}, f32[4,8,256]{2,1,0:T(8,128)S(1)}, f32[96,1024]{1,0:T(8,128)S(1)}) custom-call(f32[96,1024]{1,0:T(8,128)S(1)} %copy-done.2, f32[96,256]{1,0:T(8,128)S(1)} %copy-done.3, bf16[1,4,256,256]{3,2,1,0:T(8,128)(2,1)S(1)} %copy-done, ...), custom_call_target="tpu_custom_call" | custom-call | tf_op jit(solution)/shard_map/pallas_call | solution.py:325
  22.3 0.0 copy-done.1
  22.3 2.1 %shard_map.79 = (f32[96,1024]{1,0:T(8,128)}, f32[96,256]{1,0:T(8,128)}) custom-call(f32[96,1024]{1,0:T(8,128)S(1)} %get-tuple-element.13.smoothed, f32[4,8,256]{2,1,0:T(8,128)S(1)} %get-tuple-element.14.terms, bf16[1,4,256,256]{3,2,1,0:T(8,128)(2,1)S(1)} %copy-done.1, s32[1,4]{1,0:T(1,128)S(1)} %copy-done.5, s32[4,8]{1,0:T(4,128)S(1)} %bitcast.2, ...), custom_call_target="tpu_custom_call" | custom-call | tf_op jit(solution)/shard_map/pallas_call | solution.py:345
Async XLA Ops:
  0.6 0.7 %copy-start.6 = (s32[8]{0:T(128)S(1)}, s32[8]{0:T(128)}, u32[]{:S(2)}) copy-start(s32[8]{0:T(128)} %owner_map.3) | copy-start | bytes 100
  0.6 0.7 %copy-start.5 = (s32[1,4]{1,0:T(1,128)S(1)}, s32[1,4]{1,0:T(1,128)}, u32[]{:S(2)}) copy-start(s32[1,4]{1,0:T(1,128)} %offsets.3) | copy-start | bytes 52
  1.3 1.0 %copy-start = (bf16[1,4,256,256]{3,2,1,0:T(8,128)(2,1)S(1)}, bf16[1,4,256,256]{3,2,1,0:T(8,128)(2,1)}, u32[]{:S(2)}) copy-start(bf16[1,4,256,256]{3,2,1,0:T(8,128)(2,1)} %mats.5) | copy-start | bytes 1572868
  2.3 1.0 %copy-start.2 = (f32[96,1024]{1,0:T(8,128)S(1)}, f32[96,1024]{1,0:T(8,128)}, u32[]{:S(2)}) copy-start(f32[96,1024]{1,0:T(8,128)} %vol.3) | copy-start | bytes 1179652
  3.3 0.7 %copy-start.4 = (s32[8,4]{0,1:T(4,128)S(1)}, s32[8,4]{0,1:T(4,128)}, u32[]{:S(2)}) copy-start(s32[8,4]{0,1:T(4,128)} %param.10) | copy-start | bytes 388
  4.0 1.1 %copy-start.3 = (f32[96,256]{1,0:T(8,128)S(1)}, f32[96,256]{1,0:T(8,128)}, u32[]{:S(2)}) copy-start(f32[96,256]{1,0:T(8,128)} %sino.1) | copy-start | bytes 294916
  5.1 17.2 %copy-start.1 = (bf16[1,4,256,256]{3,2,1,0:T(8,128)(2,1)S(1)}, bf16[1,4,256,256]{3,2,1,0:T(8,128)(2,1)}, u32[]{:S(2)}) copy-start(bf16[1,4,256,256]{3,2,1,0:T(8,128)(2,1)} %mats.5) | copy-start | bytes 1572868

commit v3 on v2

--- a/solution.py
+++ b/solution.py
@@ -13,7 +13,7 @@
 
 LANES = 128
 TILE = 8
-CHUNKS = 3
+CHUNKS = 2
 TERMS = 3
 
 

time: 24.6 us -> 25.1 us (1.020)
  Pallas kernels: 20.3 us -> 20.8 us
    pallas_call x1, Pallas kernels: 17.1 us -> 17.6 us  [per_device(): pl.pallas_call(functools.partial(exchange_kernel, cfg), out_shape=tuple((...]
where the time goes in v3:
time: 25.1 us; the launch traced here: 24.9 us
  Pallas kernels  20.8 us (83%)
  local copies, waits for them, and re-layouts  3.38 us (13%)
  between operations  0.69 us (3%)
    pallas_call x1, Pallas kernels, per_device(): pl.pallas_call(functools.partial(exchange_kernel, cfg), out_shape=tuple((...  17.6 us
    unnamed x14, local copies, waits for them, and re-layouts  3.38 us
    pallas_call x1, Pallas kernels, per_device(): pl.pallas_call(functools.partial(back_kernel, cfg), out_shape=(shape(dept...  2.11 us
    pallas_call x1, Pallas kernels, per_device(): pl.pallas_call(functools.partial(project_kernel, cfg), out_shape=tuple((s...  1.09 us

profile of v3, /device:TPU:0, one launch (start us, length us, event | category | flops | bytes accessed | tf_op | source)
XLA Modules:
  0.0 24.9 jit_solution(1967490045090740567)
XLA Ops:
  0.6 0.0 copy-start.6
  0.6 0.0 copy-start.5
  0.7 0.6 %copy-done.6 = s32[8]{0:T(128)S(1)} copy-done((s32[8]{0:T(128)S(1)}, s32[8]{0:T(128)}, u32[]{:S(2)}) %copy-start.6) | copy-done | bytes 56
  1.3 0.0 copy-done.5
  1.3 0.0 copy-start
  1.3 1.0 %copy-done = bf16[1,4,256,256]{3,2,1,0:T(8,128)(2,1)S(1)} copy-done((bf16[1,4,256,256]{3,2,1,0:T(8,128)(2,1)S(1)}, bf16[1,4,256,256]{3,2,1,0:T(8,128)(2,1)}, u32[]{:S(2)}) %copy-start) | copy-done | bytes 524312
  2.3 0.0 copy-start.2
  2.3 1.0 %copy-done.2 = f32[96,1024]{1,0:T(8,128)S(1)} copy-done((f32[96,1024]{1,0:T(8,128)S(1)}, f32[96,1024]{1,0:T(8,128)}, u32[]{:S(2)}) %copy-start.2) | copy-done | bytes 393240
  3.3 0.0 copy-start.4
  3.3 0.7 %copy-done.4 = s32[8,4]{0,1:T(4,128)S(1)} copy-done((s32[8,4]{0,1:T(4,128)S(1)}, s32[8,4]{0,1:T(4,128)}, u32[]{:S(2)}) %copy-start.4) | copy-done | bytes 152
  4.0 0.0 copy-start.3
  4.0 1.1 %shard_map.77 = (f32[8,56,256]{2,1,0:T(8,128)S(1)}, f32[8,48,256]{2,1,0:T(8,128)S(1)}) custom-call(f32[96,1024]{1,0:T(8,128)S(1)} %copy-done.2, bf16[1,4,256,256]{3,2,1,0:T(8,128)(2,1)S(1)} %copy-done, s32[1,4]{1,0:T(1,128)S(1)} %copy-done.5, s32[4,8]{1,0:T(4,128)S(1)} %bitcast.1, s32[8]{0:T(128)S(1)} %copy-done.6), custom_call_target="tpu_custom_call" | custom-call | tf_op jit(solution)/shard_map/pallas_call | solution.py:316
  5.1 0.0 copy-done.3
  5.1 0.0 copy-start.1
  5.1 17.6 %shard_map.78 = (f32[8,48,256]{2,1,0:T(8,128)S(1)}, f32[8,48,256]{2,1,0:T(8,128)S(1)}, f32[4,8,256]{2,1,0:T(8,128)S(1)}, f32[96,1024]{1,0:T(8,128)S(1)}) custom-call(f32[96,1024]{1,0:T(8,128)S(1)} %copy-done.2, f32[96,256]{1,0:T(8,128)S(1)} %copy-done.3, bf16[1,4,256,256]{3,2,1,0:T(8,128)(2,1)S(1)} %copy-done, f32[8,56,256]{2,1,0:T(8,128)S(1)} %get-tuple-element.8.refs_0_, ...), custom_call_target="tpu_custom_call" | custom-call | tf_op jit(solution)/shard_map/pallas_call | solution.py:325
  22.7 0.0 copy-done.1
  22.7 2.1 %shard_map.79 = (f32[96,1024]{1,0:T(8,128)}, f32[96,256]{1,0:T(8,128)}) custom-call(f32[96,1024]{1,0:T(8,128)S(1)} %get-tuple-element.10.smoothed, f32[4,8,256]{2,1,0:T(8,128)S(1)} %get-tuple-element.11.terms, bf16[1,4,256,256]{3,2,1,0:T(8,128)(2,1)S(1)} %copy-done.1, s32[1,4]{1,0:T(1,128)S(1)} %copy-done.5, s32[4,8]{1,0:T(4,128)S(1)} %bitcast.2, ...), custom_call_target="tpu_custom_call" | custom-call | tf_op jit(solution)/shard_map/pallas_call | solution.py:345
Async XLA Ops:
  0.6 0.7 %copy-start.6 = (s32[8]{0:T(128)S(1)}, s32[8]{0:T(128)}, u32[]{:S(2)}) copy-start(s32[8]{0:T(128)} %owner_map.3) | copy-start | bytes 100
  0.6 0.7 %copy-start.5 = (s32[1,4]{1,0:T(1,128)S(1)}, s32[1,4]{1,0:T(1,128)}, u32[]{:S(2)}) copy-start(s32[1,4]{1,0:T(1,128)} %offsets.3) | copy-start | bytes 52
  1.3 1.0 %copy-start = (bf16[1,4,256,256]{3,2,1,0:T(8,128)(2,1)S(1)}, bf16[1,4,256,256]{3,2,1,0:T(8,128)(2,1)}, u32[]{:S(2)}) copy-start(bf16[1,4,256,256]{3,2,1,0:T(8,128)(2,1)} %mats.5) | copy-start | bytes 1572868
  2.3 1.0 %copy-start.2 = (f32[96,1024]{1,0:T(8,128)S(1)}, f32[96,1024]{1,0:T(8,128)}, u32[]{:S(2)}) copy-start(f32[96,1024]{1,0:T(8,128)} %vol.3) | copy-start | bytes 1179652
  3.3 0.7 %copy-start.4 = (s32[8,4]{0,1:T(4,128)S(1)}, s32[8,4]{0,1:T(4,128)}, u32[]{:S(2)}) copy-start(s32[8,4]{0,1:T(4,128)} %param.10) | copy-start | bytes 388
  4.0 1.1 %copy-start.3 = (f32[96,256]{1,0:T(8,128)S(1)}, f32[96,256]{1,0:T(8,128)}, u32[]{:S(2)}) copy-start(f32[96,256]{1,0:T(8,128)} %sino.1) | copy-start | bytes 294916
  5.1 17.6 %copy-start.1 = (bf16[1,4,256,256]{3,2,1,0:T(8,128)(2,1)S(1)}, bf16[1,4,256,256]{3,2,1,0:T(8,128)(2,1)}, u32[]{:S(2)}) copy-start(bf16[1,4,256,256]{3,2,1,0:T(8,128)(2,1)} %mats.5) | copy-start | bytes 1572868
